TPU v7x, 32 devices: a whole 2x2x4 slice. The times are simulated.
32 devices in a mesh: groups: 2 (over x), view: 2 (over core), tile: 8 (over z, y).
Axes of the slice: x: 2, y: 2, z: 4, core: 2. Of those that a mesh axis runs over, the one named last changes fastest.
Arguments:
- features: bfloat16 [8, 64, 320, 128], P(('groups', 'view'), 'tile'), parts along dimension 0, may hold values from -6 to 6
- ref_views: int32 [8], P('groups'), parts along dimension 0, may hold values from 0 to 3, as said below
- intersection: int32 [8, 4], P('groups'), parts along dimension 0, may hold values from 0 to 1, as said below
- offsets: int32 [8, 4], P('groups'), parts along dimension 0, may hold values from 0 to 16, as said below
- conv_weight: bfloat16 [3, 3, 3, 32, 40], replicated, may hold values from -0.1875 to 0.1875
- conv_bias: float32 [32], replicated, may hold values from -1.5 to 1.5
Outputs:
- regularized: bfloat16 [8, 32, 32, 64, 128], P('groups', None, 'view', 'tile'), parts along dimension 0
There are 2 independent parts, one for each index of `groups`. A program takes and returns all parts, laid end to end along the dimension named above; an argument that names none is the same for every part. Nothing has to cross between parts.
Inputs may be any that keep to these rules, and one draw needn't show every extreme that they name: `ref_views`: distinct views. `intersection`: never 1 at the reference's own view; every row has at least one source. `offsets`: the value 17 - 1 is taken at some source of some reference.
All inputs are finite; a program needn't handle non-finite values.
Results may differ from a plain program's by a relative error of at most 0.006.
Values may be sent and summed in bfloat16 or wider, within the bound.
A program may use at most 192 MiB of HBM per device.

v0:
```python
import jax
import jax.numpy as jnp
from jax import lax
from jax.sharding import PartitionSpec as P

ND = 32
OFF = 17


def passed_along(value, axis, steps):
    count = lax.axis_size(axis)
    first, last = (max(0, -steps), min(count, count - steps))
    return lax.ppermute(value, axis, [(source, source + steps) for source in range(first, last)])


def from_root(x, axis, root):
    mine = lax.axis_index(axis) == root
    return lax.psum(jnp.where(mine, x, jnp.zeros_like(x)), axis)


def padded_2(cells, sides, width):
    for axis, dim in sides:
        count = lax.axis_size(axis)
        ends = count - 1
        head = lax.slice_in_dim(cells, 0, width, axis=dim)
        tail = lax.slice_in_dim(cells, cells.shape[dim] - width, cells.shape[dim], axis=dim)
        cells = jnp.concatenate(
            [
                lax.ppermute(tail, axis, [(i, (i + 1) % count) for i in range(ends)]),
                cells,
                lax.ppermute(head, axis, [((i + 1) % count, i) for i in range(ends)]),
            ],
            axis=dim,
        )
    return cells


def group_products(reference_rows, source_rows, groups):
    rows, channels, columns = reference_rows.shape
    product = reference_rows.astype(jnp.float32) * source_rows.astype(jnp.float32)
    summed = jnp.sum(product.reshape(rows, groups, channels // groups, columns), axis=2)
    return jnp.transpose(summed, (1, 0, 2)) * (1.0 / (channels // groups))


def correlate(reference_rows, window, groups, depth):
    rows = reference_rows.shape[0]
    layers = [
        group_products(
            reference_rows, window[depth - 1 - disparity : depth - 1 - disparity + rows], groups
        )
        for disparity in range(depth)
    ]
    return jnp.stack(layers, axis=1)


def regularize(padded, conv_weight, conv_bias):
    groups, depth_pad, rows_pad, columns = padded.shape
    depth = depth_pad - 2
    rows = rows_pad - 2
    channels_out = conv_weight.shape[3]
    widened = jnp.pad(padded, ((0, 0), (0, 0), (0, 0), (1, 1)))
    stacked = jnp.concatenate(
        [
            widened[:, :, row_tap : row_tap + rows, column_tap : column_tap + columns]
            for row_tap in range(3)
            for column_tap in range(3)
        ],
        axis=0,
    )
    total = jnp.zeros((channels_out, depth, rows, columns), jnp.float32)
    for depth_tap in range(3):
        tap_matrix = jnp.transpose(conv_weight[depth_tap], (2, 0, 1, 3)).reshape(
            channels_out, 9 * groups
        )
        total = total + jnp.einsum(
            "ok,kdrw->odrw",
            tap_matrix,
            stacked[:, depth_tap : depth_tap + depth],
            preferred_element_type=jnp.float32,
        )
    return jax.nn.relu(total + conv_bias[:, None, None, None]).astype(jnp.bfloat16)


def shards(features, ref_views, intersection, offsets, conv_weight, conv_bias):
    local_views, rows, channels, columns = features.shape
    groups = conv_weight.shape[4]
    depth = ND
    reach = ND + OFF - 1
    blocks = (reach + rows - 1) // rows
    pieces = []
    for distance in range(blocks, 0, -1):
        pieces.append(passed_along(features, "tile", distance))
    lower = jnp.concatenate(pieces, axis=1)
    extended = jnp.concatenate([lower, features], axis=1)
    view_index = lax.axis_index("view")
    results = []
    for slot in range(ref_views.shape[0]):
        target = ref_views[slot]
        owned = lax.dynamic_index_in_dim(features, target % local_views, 0, keepdims=False)
        reference_rows = from_root(owned, "view", target // local_views)
        partial_value = jnp.zeros((groups, depth, rows, columns), jnp.float32)
        for inner in range(local_views):
            view = view_index * local_views + inner
            start = blocks * rows - offsets[slot, view] - (depth - 1)
            window = lax.dynamic_slice_in_dim(extended[inner], start, rows + depth - 1, 0)
            partial_value = partial_value + intersection[slot, view].astype(
                jnp.float32
            ) * correlate(reference_rows, window, groups, depth)
        scale = 1.0 / jnp.sum(intersection[slot]).astype(jnp.float32)
        shares = lax.psum_scatter(
            partial_value.astype(jnp.bfloat16), "view", scatter_dimension=1, tiled=True
        ).astype(jnp.float32)
        cost = (shares * scale).astype(jnp.bfloat16)
        padded = padded_2(cost, (("view", 1), ("tile", 2)), 1)
        results.append(regularize(padded, conv_weight, conv_bias))
    return jnp.stack(results, axis=0)


def solution(mesh):
    placed = (
        P(("groups", "view"), "tile", None, None),
        P("groups"),
        P("groups", None),
        P("groups", None),
        P(),
        P(),
    )
    return jax.shard_map(
        shards,
        mesh=mesh,
        in_specs=placed,
        out_specs=P("groups", None, "view", "tile", None),
        check_vma=False,
    )
```

profile of v0, /device:TPU:24, one launch (start us, length us, event | category | flops | bytes accessed | tf_op | source)
XLA Modules:
  0.0 639.6 jit_solution(18227853094817527776)
XLA Ops:
  28.0 14.5 %collective-permute-done = bf16[2,8,320,128]{3,2,1,0:T(8,128)(2,1)} collective-permute-done((bf16[2,8,320,128]{3,2,1,0:T(8,128)(2,1)}, bf16[2,8,320,128]{3,2,1,0:T(8,128)(2,1)}, u32[]{:S(2)}, u32[]{:S(2)}) %collective-permute-start) | collective-permute-done | bytes 1310752 | tf_op jit(solution)/shard_map/ppermute | solution.py:13
  62.9 8.6 %collective-permute-done.1 = bf16[2,8,320,128]{3,2,1,0:T(8,128)(2,1)} collective-permute-done((bf16[2,8,320,128]{3,2,1,0:T(8,128)(2,1)}, bf16[2,8,320,128]{3,2,1,0:T(8,128)(2,1)}, u32[]{:S(2)}, u32[]{:S(2)}) %collective-permute-start.1) | collective-permute-done | bytes 1310752 | tf_op jit(solution)/shard_map/ppermute | solution.py:13
  73.0 80.7 %collective-permute-done.2 = bf16[2,8,320,128]{3,2,1,0:T(8,128)(2,1)} collective-permute-done((bf16[2,8,320,128]{3,2,1,0:T(8,128)(2,1)S(1)}, bf16[2,8,320,128]{3,2,1,0:T(8,128)(2,1)}, u32[]{:S(2)}, u32[]{:S(2)}) %collective-permute-start.2) | collective-permute-done | bytes 1310752 | tf_op jit(solution)/shard_map/ppermute | solution.py:13
  155.2 27.5 %collective-permute-done.3 = bf16[2,8,320,128]{3,2,1,0:T(8,128)(2,1)} collective-permute-done((bf16[2,8,320,128]{3,2,1,0:T(8,128)(2,1)S(1)}, bf16[2,8,320,128]{3,2,1,0:T(8,128)(2,1)}, u32[]{:S(2)}, u32[]{:S(2)}) %collective-permute-start.3) | collective-permute-done | bytes 1310752 | tf_op jit(solution)/shard_map/ppermute | solution.py:13
  191.6 10.0 %fusion.79 = (f32[8,40,128]{2,1,0:T(8,128)S(1)}, f32[8,40,128]{2,1,0:T(8,128)S(1)}, f32[8,40,128]{2,1,0:T(8,128)S(1)}, f32[8,40,128]{2,1,0:T(8,128)S(1)}, f32[8,...) fusion(bf16[8,320,128]{2,1,0:T(8,128)(2,1)} %get-tuple-element., ...), kind=kLoop, calls=%fused_computation.416 | loop fusion | flops 14458880 | bytes 12943420 | tf_op jit(solution)/shard_map/reduce_sum | solution.py:41
  201.7 7.6 %fusion.145 = (f32[8,40,128]{2,1,0:T(8,128)S(1)}, f32[8,40,128]{2,1,0:T(8,128)S(1)}, f32[8,40,128]{2,1,0:T(8,128)S(1)}, f32[8,40,128]{2,1,0:T(8,128)S(1)}, f32[8...) fusion(bf16[8,320,128]{2,1,0:T(8,128)(2,1)S(1)} %copy-done.11, ...), kind=kLoop, calls=%fused_computation.482 | loop fusion | flops 16343040 | bytes 14581828 | tf_op jit(solution)/shard_map/reduce_sum | solution.py:41
  209.3 7.7 %fusion.81 = (f32[8,40,128]{2,1,0:T(8,128)S(1)}, f32[8,40,128]{2,1,0:T(8,128)S(1)}, f32[8,40,128]{2,1,0:T(8,128)S(1)}, f32[8,40,128]{2,1,0:T(8,128)S(1)}, f32[8,...) fusion(bf16[8,320,128]{2,1,0:T(8,128)(2,1)S(1)} %copy-done.11, ...), kind=kLoop, calls=%fused_computation.418 | loop fusion | flops 16343040 | bytes 14581828 | tf_op jit(solution)/shard_map/reduce_sum | solution.py:41
  227.8 10.6 %fusion.207 = (f32[8,40,128]{2,1,0:T(8,128)S(1)}, f32[8,40,128]{2,1,0:T(8,128)}, f32[8,40,128]{2,1,0:T(8,128)}, f32[8,40,128]{2,1,0:T(8,128)}, f32[8,40,128]{2,1...) fusion(bf16[8,320,128]{2,1,0:T(8,128)(2,1)S(1)} %copy-done.10, ...), kind=kLoop, calls=%fused_computation.544 | loop fusion | flops 14458880 | bytes 12943420 | tf_op jit(solution)/shard_map/reduce_sum | solution.py:41
  238.4 7.6 %fusion.273 = (f32[8,40,128]{2,1,0:T(8,128)S(1)}, f32[8,40,128]{2,1,0:T(8,128)S(1)}, f32[8,40,128]{2,1,0:T(8,128)S(1)}, f32[8,40,128]{2,1,0:T(8,128)S(1)}, f32[8...) fusion(bf16[8,320,128]{2,1,0:T(8,128)(2,1)S(1)} %copy-done.10, ...), kind=kLoop, calls=%fused_computation.610 | loop fusion | flops 16343040 | bytes 14581828 | tf_op jit(solution)/shard_map/reduce_sum | solution.py:41
  246.0 7.7 %fusion.335 = (f32[8,40,128]{2,1,0:T(8,128)}, f32[8,40,128]{2,1,0:T(8,128)}, f32[8,40,128]{2,1,0:T(8,128)}, f32[8,40,128]{2,1,0:T(8,128)}, f32[8,40,128]{2,1,0:T...) fusion(bf16[8,320,128]{2,1,0:T(8,128)(2,1)S(1)} %copy-done.9, ...), kind=kLoop, calls=%fused_computation.672 | loop fusion | flops 14458880 | bytes 12943420 | tf_op jit(solution)/shard_map/reduce_sum | solution.py:41
  254.4 9.3 %fusion.401 = (f32[8,40,128]{2,1,0:T(8,128)}, f32[8,40,128]{2,1,0:T(8,128)S(1)}, f32[8,40,128]{2,1,0:T(8,128)}, f32[8,40,128]{2,1,0:T(8,128)}, f32[8,40,128]{2,1...) fusion(bf16[8,320,128]{2,1,0:T(8,128)(2,1)S(1)} %copy-done.9, ...), kind=kLoop, calls=%fused_computation.738 | loop fusion | flops 16343040 | bytes 14581828 | tf_op jit(solution)/shard_map/reduce_sum | solution.py:41
  264.5 7.7 %fusion.463 = (f32[8,40,128]{2,1,0:T(8,128)}, f32[8,40,128]{2,1,0:T(8,128)}, f32[8,40,128]{2,1,0:T(8,128)}, f32[8,40,128]{2,1,0:T(8,128)}, f32[8,40,128]{2,1,0:T...) fusion(bf16[8,320,128]{2,1,0:T(8,128)(2,1)S(1)} %copy-done.8, ...), kind=kLoop, calls=%fused_computation.800 | loop fusion | flops 14458880 | bytes 12943420 | tf_op jit(solution)/shard_map/reduce_sum | solution.py:41
  272.8 8.4 %fusion.529 = (f32[8,40,128]{2,1,0:T(8,128)S(1)}, f32[8,40,128]{2,1,0:T(8,128)S(1)}, f32[8,40,128]{2,1,0:T(8,128)}, f32[8,40,128]{2,1,0:T(8,128)}, f32[8,40,128]...) fusion(bf16[8,320,128]{2,1,0:T(8,128)(2,1)S(1)} %copy-done.8, ...), kind=kLoop, calls=%fused_computation.866 | loop fusion | flops 16343040 | bytes 14581828 | tf_op jit(solution)/shard_map/reduce_sum | solution.py:41
  281.9 7.7 %fusion.209 = (f32[8,40,128]{2,1,0:T(8,128)S(1)}, f32[8,40,128]{2,1,0:T(8,128)S(1)}, f32[8,40,128]{2,1,0:T(8,128)S(1)}, f32[8,40,128]{2,1,0:T(8,128)S(1)}, f32[8...) fusion(bf16[8,320,128]{2,1,0:T(8,128)(2,1)S(1)} %copy-done.10, ...), kind=kLoop, calls=%fused_computation.546 | loop fusion | flops 16343040 | bytes 14581828 | tf_op jit(solution)/shard_map/reduce_sum | solution.py:41
  301.0 10.6 %fusion.337 = (f32[8,40,128]{2,1,0:T(8,128)S(1)}, f32[8,40,128]{2,1,0:T(8,128)S(1)}, f32[8,40,128]{2,1,0:T(8,128)S(1)}, f32[8,40,128]{2,1,0:T(8,128)S(1)}, f32[8...) fusion(bf16[8,320,128]{2,1,0:T(8,128)(2,1)S(1)} %copy-done.9, ...), kind=kLoop, calls=%fused_computation.674 | loop fusion | flops 16343040 | bytes 14581828 | tf_op jit(solution)/shard_map/reduce_sum | solution.py:41
  343.0 6.7 %fusion.399 = (f32[8,40,128]{2,1,0:T(8,128)S(1)}, f32[8,40,128]{2,1,0:T(8,128)S(1)}, f32[8,40,128]{2,1,0:T(8,128)S(1)}, f32[8,40,128]{2,1,0:T(8,128)S(1)}, f32[8...) fusion(bf16[8,320,128]{2,1,0:T(8,128)(2,1)S(1)} %copy-done.9, ...), kind=kLoop, calls=%fused_computation.736 | loop fusion | flops 14458880 | bytes 12943420 | tf_op jit(solution)/shard_map/reduce_sum | solution.py:41
  352.7 11.0 %fusion.465 = (f32[8,40,128]{2,1,0:T(8,128)S(1)}, f32[8,40,128]{2,1,0:T(8,128)S(1)}, f32[8,40,128]{2,1,0:T(8,128)S(1)}, f32[8,40,128]{2,1,0:T(8,128)S(1)}, f32[8...) fusion(bf16[8,320,128]{2,1,0:T(8,128)(2,1)S(1)} %copy-done.8, ...), kind=kLoop, calls=%fused_computation.802 | loop fusion | flops 16343040 | bytes 14581828 | tf_op jit(solution)/shard_map/reduce_sum | solution.py:41
  395.1 6.7 %fusion.527 = (f32[8,40,128]{2,1,0:T(8,128)S(1)}, f32[8,40,128]{2,1,0:T(8,128)S(1)}, f32[8,40,128]{2,1,0:T(8,128)S(1)}, f32[8,40,128]{2,1,0:T(8,128)S(1)}, f32[8...) fusion(bf16[8,320,128]{2,1,0:T(8,128)(2,1)S(1)} %copy-done.8, ...), kind=kLoop, calls=%fused_computation.864 | loop fusion | flops 14458880 | bytes 12943420 | tf_op jit(solution)/shard_map/reduce_sum | solution.py:41
  426.3 41.2 %reduce-scatter.11.cloned.1.call-done = bf16[40,16,8,128]{3,0,2,1:T(8,128)(2,1)} async-done(((bf16[40,32,8,128]{3,0,2,1:T(8,128)(2,1)}), bf16[40,16,8,128]{3,0,2,1:T(8,128)(2,1)}) %reduce-scatter.11.cloned.1.call-update) | async-done | bytes 1310736 | tf_op jit(solution)/shard_map/reduce_scatter | solution.py:110
  486.4 12.4 %collective-permute-start.13 = (bf16[40,18,1,128]{3,0,2,1:T(8,128)(2,1)S(1)}, bf16[40,18,1,128]{3,0,2,1:T(8,128)(2,1)S(1)}, u32[]{:S(2)}, u32[]{:S(2)}) collective-permute-start(bf16[40,18,1,128]{3,0,2,1:T(8,128)(2,1)S(1)} %get-tuple-element.274), channel_id=1, source_target_pairs={{1,0},{2,1},{3,2},{4,3},{5,4},{6,5},{7,6},{9,8},{10,9},{11,10},{12... | collective-permute-start | bytes 552968 | tf_op jit(solution)/shard_map/ppermute | solution.py:31
  559.6 7.6 %fusion.536 = f32[16,8,128,32]{2,3,1,0:T(8,128)} fusion(bf16[360,18,8,128]{3,0,2,1:T(8,128)(2,1)} %slice_dynamic-update-slice_fusion.6, bf16[32,360,1,1]{1,0,2,3:T(8,128)(2,1)S(1)} %reshape.2131), kind=kOutput, calls=%fused_computation.1407 | convolution fusion | flops 377487360 | bytes 15391232 | tf_op jit(solution)/shard_map/ok,kdrw->odrw/dot_general | solution.py:75
  567.2 7.6 %fusion.544 = f32[16,8,128,32]{2,3,1,0:T(8,128)} fusion(bf16[360,18,8,128]{3,0,2,1:T(8,128)(2,1)} %slice_dynamic-update-slice_fusion.6, bf16[32,360,1,1]{1,0,2,3:T(8,128)(2,1)S(1)} %copy-done.70), kind=kOutput, calls=%fused_computation.1415 | convolution fusion | flops 377487360 | bytes 15391232 | tf_op jit(solution)/shard_map/ok,kdrw->odrw/dot_general | solution.py:75
  593.1 7.6 %fusion.534 = f32[16,8,128,32]{2,3,1,0:T(8,128)} fusion(bf16[360,18,8,128]{3,0,2,1:T(8,128)(2,1)} %slice_dynamic-update-slice_fusion, bf16[32,360,1,1]{1,0,2,3:T(8,128)(2,1)S(1)} %reshape.2131), kind=kOutput, calls=%fused_computation.1405 | convolution fusion | flops 377487360 | bytes 15391232 | tf_op jit(solution)/shard_map/ok,kdrw->odrw/dot_general | solution.py:75
  600.7 7.7 %fusion.542 = f32[16,8,128,32]{2,3,1,0:T(8,128)} fusion(bf16[360,18,8,128]{3,0,2,1:T(8,128)(2,1)} %slice_dynamic-update-slice_fusion, bf16[32,360,1,1]{1,0,2,3:T(8,128)(2,1)S(1)} %copy-done.70), kind=kOutput, calls=%fused_computation.1413 | convolution fusion | flops 377487360 | bytes 15391232 | tf_op jit(solution)/shard_map/ok,kdrw->odrw/dot_general | solution.py:75
  (590 shorter events, 261.1 us)
Async XLA Ops:
  6.5 185.0 %all-reduce.7.cloned.1.call-start = ((), (), s32[]{:S(2)}) async-start(), calls=%async_computation.8 | async-start | bytes 5242880 | tf_op jit(solution)/shard_map/psum | solution.py:18
  6.5 35.9 %collective-permute-start = (bf16[2,8,320,128]{3,2,1,0:T(8,128)(2,1)}, bf16[2,8,320,128]{3,2,1,0:T(8,128)(2,1)}, u32[]{:S(2)}, u32[]{:S(2)}) collective-permute-start(bf16[2,8,320,128]{3,2,1,0:T(8,128)(2,1)} %param.6), channel_id=1, source_target_pairs={{0,6},{1,7},{8,14},{9,15},{16,22},{17,23},{24,30},{25,31}} | collective-permute-start | bytes 3932168 | tf_op jit(solution)/shard_map/ppermute | solution.py:13
  8.0 63.6 %collective-permute-start.1 = (bf16[2,8,320,128]{3,2,1,0:T(8,128)(2,1)}, bf16[2,8,320,128]{3,2,1,0:T(8,128)(2,1)}, u32[]{:S(2)}, u32[]{:S(2)}) collective-permute-start(bf16[2,8,320,128]{3,2,1,0:T(8,128)(2,1)} %param.6), channel_id=1, source_target_pairs={{0,5},{1,6},{2,7},{8,13},{9,14},{10,15},{16,21},{17,22},{18,23},{2... | collective-permute-start | bytes 3932168 | tf_op jit(solution)/shard_map/ppermute | solution.py:13
  24.0 384.8 %reduce-scatter.5.cloned.1.call-start = ((), (), s32[]{:S(2)}) async-start(), calls=%async_computation.4 | async-start | bytes 3932160 | tf_op jit(solution)/shard_map/reduce_scatter | solution.py:110
  24.1 129.6 %collective-permute-start.2 = (bf16[2,8,320,128]{3,2,1,0:T(8,128)(2,1)S(1)}, bf16[2,8,320,128]{3,2,1,0:T(8,128)(2,1)}, u32[]{:S(2)}, u32[]{:S(2)}) collective-permute-start(bf16[2,8,320,128]{3,2,1,0:T(8,128)(2,1)S(1)} %copy-done.7), channel_id=1, source_target_pairs={{0,4},{1,5},{2,6},{3,7},{8,12},{9,13},{10,14},{11,15},{16,20},{17,... | collective-permute-start | bytes 3932168 | tf_op jit(solution)/shard_map/ppermute | solution.py:13
  25.4 157.4 %collective-permute-start.3 = (bf16[2,8,320,128]{3,2,1,0:T(8,128)(2,1)S(1)}, bf16[2,8,320,128]{3,2,1,0:T(8,128)(2,1)}, u32[]{:S(2)}, u32[]{:S(2)}) collective-permute-start(bf16[2,8,320,128]{3,2,1,0:T(8,128)(2,1)S(1)} %copy-done.7), channel_id=1, source_target_pairs={{0,3},{1,4},{2,5},{3,6},{4,7},{8,11},{9,12},{10,13},{11,14},{12,15... | collective-permute-start | bytes 3932168 | tf_op jit(solution)/shard_map/ppermute | solution.py:13
  26.7 157.6 %collective-permute-start.4 = (bf16[2,8,320,128]{3,2,1,0:T(8,128)(2,1)S(1)}, bf16[2,8,320,128]{3,2,1,0:T(8,128)(2,1)}, u32[]{:S(2)}, u32[]{:S(2)}) collective-permute-start(bf16[2,8,320,128]{3,2,1,0:T(8,128)(2,1)S(1)} %copy-done.7), channel_id=1, source_target_pairs={{0,2},{1,3},{2,4},{3,5},{4,6},{5,7},{8,10},{9,11},{10,12},{11,13},... | collective-permute-start | bytes 3932168 | tf_op jit(solution)/shard_map/ppermute | solution.py:13
  42.5 143.3 %collective-permute-start.5 = (bf16[2,8,320,128]{3,2,1,0:T(8,128)(2,1)S(1)}, bf16[2,8,320,128]{3,2,1,0:T(8,128)(2,1)}, u32[]{:S(2)}, u32[]{:S(2)}) collective-permute-start(bf16[2,8,320,128]{3,2,1,0:T(8,128)(2,1)S(1)} %copy-done.7), channel_id=1, source_target_pairs={{0,1},{1,2},{2,3},{3,4},{4,5},{5,6},{6,7},{8,9},{9,10},{10,11},{11... | collective-permute-start | bytes 3932168 | tf_op jit(solution)/shard_map/ppermute | solution.py:13
  227.7 187.1 %reduce-scatter.7.cloned.1.call-start = ((), (), s32[]{:S(2)}) async-start(), calls=%async_computation.5 | async-start | bytes 3932160 | tf_op jit(solution)/shard_map/reduce_scatter | solution.py:110
  301.0 119.9 %reduce-scatter.9.cloned.1.call-start = ((), (), s32[]{:S(2)}) async-start(), calls=%async_computation.6 | async-start | bytes 3932160 | tf_op jit(solution)/shard_map/reduce_scatter | solution.py:110
  352.7 114.8 %reduce-scatter.11.cloned.1.call-start = ((), (), s32[]{:S(2)}) async-start(), calls=%async_computation.7 | async-start | bytes 3932160 | tf_op jit(solution)/shard_map/reduce_scatter | solution.py:110
  411.6 57.6 %collective-permute-start.6 = (bf16[40,1,8,128]{3,0,2,1:T(8,128)(2,1)S(1)}, bf16[40,1,8,128]{3,0,2,1:T(8,128)(2,1)S(1)}, u32[]{:S(2)}, u32[]{:S(2)}) collective-permute-start(bf16[40,1,8,128]{3,0,2,1:T(8,128)(2,1)S(1)} %get-tuple-element.279), channel_id=1, source_target_pairs={{0,8},{1,9},{2,10},{3,11},{4,12},{5,13},{6,14},{7,15},{16,24},{17,... | collective-permute-start | bytes 245768 | tf_op jit(solution)/shard_map/ppermute | solution.py:29
  413.5 57.1 %collective-permute-start.7 = (bf16[40,1,8,128]{3,0,2,1:T(8,128)(2,1)S(1)}, bf16[40,1,8,128]{3,0,2,1:T(8,128)(2,1)S(1)}, u32[]{:S(2)}, u32[]{:S(2)}) collective-permute-start(bf16[40,1,8,128]{3,0,2,1:T(8,128)(2,1)S(1)} %get-tuple-element.280), channel_id=1, source_target_pairs={{8,0},{9,1},{10,2},{11,3},{12,4},{13,5},{14,6},{15,7},{24,16},{25,... | collective-permute-start | bytes 245768 | tf_op jit(solution)/shard_map/ppermute | solution.py:31
  416.6 58.6 %collective-permute-start.10 = (bf16[40,1,8,128]{3,0,2,1:T(8,128)(2,1)S(1)}, bf16[40,1,8,128]{3,0,2,1:T(8,128)(2,1)S(1)}, u32[]{:S(2)}, u32[]{:S(2)}) collective-permute-start(bf16[40,1,8,128]{3,0,2,1:T(8,128)(2,1)S(1)} %get-tuple-element.281), channel_id=1, source_target_pairs={{0,8},{1,9},{2,10},{3,11},{4,12},{5,13},{6,14},{7,15},{16,24},{17,... | collective-permute-start | bytes 245768 | tf_op jit(solution)/shard_map/ppermute | solution.py:29
  419.5 57.0 %collective-permute-start.11 = (bf16[40,1,8,128]{3,0,2,1:T(8,128)(2,1)S(1)}, bf16[40,1,8,128]{3,0,2,1:T(8,128)(2,1)S(1)}, u32[]{:S(2)}, u32[]{:S(2)}) collective-permute-start(bf16[40,1,8,128]{3,0,2,1:T(8,128)(2,1)S(1)} %get-tuple-element.282), channel_id=1, source_target_pairs={{8,0},{9,1},{10,2},{11,3},{12,4},{13,5},{14,6},{15,7},{24,16},{25,... | collective-permute-start | bytes 245768 | tf_op jit(solution)/shard_map/ppermute | solution.py:31
  423.2 57.1 %collective-permute-start.14 = (bf16[40,1,8,128]{3,0,2,1:T(8,128)(2,1)}, bf16[40,1,8,128]{3,0,2,1:T(8,128)(2,1)S(1)}, u32[]{:S(2)}, u32[]{:S(2)}) collective-permute-start(bf16[40,1,8,128]{3,0,2,1:T(8,128)(2,1)} %get-tuple-element.283), channel_id=1, source_target_pairs={{0,8},{1,9},{2,10},{3,11},{4,12},{5,13},{6,14},{7,15},{16,24},{17,... | collective-permute-start | bytes 245768 | tf_op jit(solution)/shard_map/ppermute | solution.py:29
  476.5 24.5 %collective-permute-start.8 = (bf16[40,18,1,128]{3,0,2,1:T(8,128)(2,1)S(1)}, bf16[40,18,1,128]{3,0,2,1:T(8,128)(2,1)S(1)}, u32[]{:S(2)}, u32[]{:S(2)}) collective-permute-start(bf16[40,18,1,128]{3,0,2,1:T(8,128)(2,1)S(1)} %get-tuple-element.271), channel_id=1, source_target_pairs={{0,1},{1,2},{2,3},{3,4},{4,5},{5,6},{6,7},{8,9},{9,10},{10,11},{11... | collective-permute-start | bytes 552968 | tf_op jit(solution)/shard_map/ppermute | solution.py:29
  480.3 25.6 %collective-permute-start.9 = (bf16[40,18,1,128]{3,0,2,1:T(8,128)(2,1)S(1)}, bf16[40,18,1,128]{3,0,2,1:T(8,128)(2,1)S(1)}, u32[]{:S(2)}, u32[]{:S(2)}) collective-permute-start(bf16[40,18,1,128]{3,0,2,1:T(8,128)(2,1)S(1)} %get-tuple-element.272), channel_id=1, source_target_pairs={{1,0},{2,1},{3,2},{4,3},{5,4},{6,5},{7,6},{9,8},{10,9},{11,10},{12... | collective-permute-start | bytes 552968 | tf_op jit(solution)/shard_map/ppermute | solution.py:31
  483.7 38.2 %collective-permute-start.12 = (bf16[40,18,1,128]{3,0,2,1:T(8,128)(2,1)S(1)}, bf16[40,18,1,128]{3,0,2,1:T(8,128)(2,1)S(1)}, u32[]{:S(2)}, u32[]{:S(2)}) collective-permute-start(bf16[40,18,1,128]{3,0,2,1:T(8,128)(2,1)S(1)} %get-tuple-element.273), channel_id=1, source_target_pairs={{0,1},{1,2},{2,3},{3,4},{4,5},{5,6},{6,7},{8,9},{9,10},{10,11},{11... | collective-permute-start | bytes 552968 | tf_op jit(solution)/shard_map/ppermute | solution.py:29
  486.4 40.5 %collective-permute-start.13 = (bf16[40,18,1,128]{3,0,2,1:T(8,128)(2,1)S(1)}, bf16[40,18,1,128]{3,0,2,1:T(8,128)(2,1)S(1)}, u32[]{:S(2)}, u32[]{:S(2)}) collective-permute-start(bf16[40,18,1,128]{3,0,2,1:T(8,128)(2,1)S(1)} %get-tuple-element.274), channel_id=1, source_target_pairs={{1,0},{2,1},{3,2},{4,3},{5,4},{6,5},{7,6},{9,8},{10,9},{11,10},{12... | collective-permute-start | bytes 552968 | tf_op jit(solution)/shard_map/ppermute | solution.py:31
  498.9 42.1 %collective-permute-start.16 = (bf16[40,18,1,128]{3,0,2,1:T(8,128)(2,1)S(1)}, bf16[40,18,1,128]{3,0,2,1:T(8,128)(2,1)S(1)}, u32[]{:S(2)}, u32[]{:S(2)}) collective-permute-start(bf16[40,18,1,128]{3,0,2,1:T(8,128)(2,1)S(1)} %get-tuple-element.275), channel_id=1, source_target_pairs={{0,1},{1,2},{2,3},{3,4},{4,5},{5,6},{6,7},{8,9},{9,10},{10,11},{11... | collective-permute-start | bytes 552968 | tf_op jit(solution)/shard_map/ppermute | solution.py:29
  501.0 39.9 %collective-permute-start.17 = (bf16[40,18,1,128]{3,0,2,1:T(8,128)(2,1)S(1)}, bf16[40,18,1,128]{3,0,2,1:T(8,128)(2,1)S(1)}, u32[]{:S(2)}, u32[]{:S(2)}) collective-permute-start(bf16[40,18,1,128]{3,0,2,1:T(8,128)(2,1)S(1)} %get-tuple-element.276), channel_id=1, source_target_pairs={{1,0},{2,1},{3,2},{4,3},{5,4},{6,5},{7,6},{9,8},{10,9},{11,10},{12... | collective-permute-start | bytes 552968 | tf_op jit(solution)/shard_map/ppermute | solution.py:31
  505.9 68.9 %collective-permute-start.20 = (bf16[40,18,1,128]{3,0,2,1:T(8,128)(2,1)S(1)}, bf16[40,18,1,128]{3,0,2,1:T(8,128)(2,1)S(1)}, u32[]{:S(2)}, u32[]{:S(2)}) collective-permute-start(bf16[40,18,1,128]{3,0,2,1:T(8,128)(2,1)S(1)} %get-tuple-element.277), channel_id=1, source_target_pairs={{0,1},{1,2},{2,3},{3,4},{4,5},{5,6},{6,7},{8,9},{9,10},{10,11},{11... | collective-permute-start | bytes 552968 | tf_op jit(solution)/shard_map/ppermute | solution.py:29
  521.9 52.9 %collective-permute-start.21 = (bf16[40,18,1,128]{3,0,2,1:T(8,128)(2,1)S(1)}, bf16[40,18,1,128]{3,0,2,1:T(8,128)(2,1)S(1)}, u32[]{:S(2)}, u32[]{:S(2)}) collective-permute-start(bf16[40,18,1,128]{3,0,2,1:T(8,128)(2,1)S(1)} %get-tuple-element.278), channel_id=1, source_target_pairs={{1,0},{2,1},{3,2},{4,3},{5,4},{6,5},{7,6},{9,8},{10,9},{11,10},{12... | collective-permute-start | bytes 552968 | tf_op jit(solution)/shard_map/ppermute | solution.py:31
  (94 other events, 1497.9 us)
Sparse Core Ops, SparseCore 0:
  24.1 26.9 all-reduce.6
  227.8 62.6 reduce-scatter.4
  301.1 62.7 reduce-scatter.6
  366.1 49.4 reduce-scatter.8
  417.7 49.7 reduce-scatter.10
where the time goes:
time: 648 us; the launch traced here: 640 us
  other arithmetic  251 us (39%)
  waiting for transfers between devices  173 us (27%)
  starting transfers between devices  61.9 us (10%)
  matrix products  61 us (9%)
  local copies, waits for them, and re-layouts  49.8 us (8%)
  between operations  43.6 us (7%)
    reduce_sum x16, other arithmetic, group_products(): jnp.sum(product.reshape(rows, groups, channels // groups, columns), axis=2)  133 us
    ppermute x6, waiting for transfers between devices, passed_along(): lax.ppermute(value, axis, [(source, source + steps) for source in range(f...  131 us
    unnamed x268, other arithmetic  76.7 us
    dot_general x12, matrix products, regularize(): jnp.einsum('ok,kdrw->odrw', tap_matrix, stacked[:, depth_tap:depth_tap +...  61 us
    reduce_scatter x4, waiting for transfers between devices, shards(): lax.psum_scatter(partial_value.astype(jnp.bfloat16), 'view', scatter_dime...  41.2 us
    unnamed x208, local copies, waits for them, and re-layouts  33.4 us
    ppermute x8, starting transfers between devices, padded_2(): lax.ppermute(head, axis, [((i + 1) % count, i) for i in range(ends)])  30.9 us
    ppermute x8, starting transfers between devices, padded_2(): lax.ppermute(tail, axis, [(i, (i + 1) % count) for i in range(ends)])  20.8 us
  transfers between devices with their start and end apart: 27, of which 5 were waited for; matrix products, arithmetic and copies ran while one was open for 42% of the time, Pallas kernels for 0%

commit v1 on v0

v1 whole, which is shorter than its diff:
```python
import functools

import jax
import jax.numpy as jnp
from jax import lax
from jax.experimental import pallas as pl
from jax.experimental.pallas import tpu as pltpu
from jax.sharding import PartitionSpec as P

ND = 32
OFF = 17
BELOW = 6
MESH = pl.DeviceIdType.MESH
PARTS = 2


def gather_kernel(count, feat, ext, zeros, local_sem, zero_sem, z_send, z_recv, pair_send, pair_recv, core_send, core_recv, edge_send, edge_recv):
    views, rows = feat.shape[0], feat.shape[1]
    tile = lax.axis_index("tile")
    core = lax.axis_index("view")
    other = 1 - core
    odd = tile % 2
    partner = tile + 1 - 2 * odd
    top = BELOW * rows
    step = rows // PARTS
    pieces = [(v, h * step) for v in range(views) for h in range(PARTS)]

    barrier = pltpu.get_barrier_semaphore()
    pl.semaphore_signal(barrier, inc=1, device_id={"view": other}, device_id_type=MESH)
    peers = jnp.int32(1)
    for shift, both in ((2, False), (-2, False), (1, True), (-1, True)):
        there = (tile + shift >= 0) & (tile + shift < count)
        peers = peers + jnp.where(there, 2 if both else 1, 0)

        @pl.when(there)
        def _(shift=shift, both=both):
            pl.semaphore_signal(barrier, inc=1, device_id={"tile": tile + shift}, device_id_type=MESH)
            if both:
                pl.semaphore_signal(barrier, inc=1, device_id={"tile": tile + shift, "view": other}, device_id_type=MESH)

    pl.semaphore_wait(barrier, peers)

    def slot(q, piece):
        v, row = piece
        return ext.at[core * views + v, pl.ds((BELOW - q) * rows + row, step)]

    def mine(piece):
        v, row = piece
        return feat.at[v, pl.ds(row, step)]

    def z_copy(p, n):
        src = mine(pieces[n]) if p == 0 else slot(2 * p, pieces[n])
        return pltpu.make_async_remote_copy(src, slot(2 * p + 2, pieces[n]), z_send.at[p, n], z_recv.at[p, n], device_id={"tile": tile + 2}, device_id_type=MESH)

    def even_copy(k, n):
        src = mine(pieces[n]) if k == 0 else slot(2 * k, pieces[n])
        return pltpu.make_async_remote_copy(src, slot(2 * k + 1, pieces[n]), pair_send.at[k, n], pair_recv.at[k, n], device_id={"tile": partner}, device_id_type=MESH)

    def odd_copy(k, n):
        return pltpu.make_async_remote_copy(slot(2 * k + 2, pieces[n]), slot(2 * k + 1, pieces[n]), pair_send.at[k, n], pair_recv.at[k, n], device_id={"tile": partner}, device_id_type=MESH)

    def core_copy(q, n):
        src = mine(pieces[n]) if q == 0 else slot(q, pieces[n])
        return pltpu.make_async_remote_copy(src, slot(q, pieces[n]), core_send.at[q, n], core_recv.at[q, n], device_id={"view": other}, device_id_type=MESH)

    def edge_copy(n):
        return pltpu.make_async_remote_copy(
            feat.at[:, pl.ds(0, 1)],
            ext.at[pl.ds(core * views, views), pl.ds(top + rows, 1)],
            edge_send.at[n],
            edge_recv.at[n],
            device_id={"tile": tile - 1} if n == 0 else {"tile": tile - 1, "view": other},
            device_id_type=MESH,
        )

    def local_copy():
        return pltpu.make_async_copy(feat, ext.at[pl.ds(core * views, views), pl.ds(top, rows)], local_sem)

    def zero_copy(q, v):
        return pltpu.make_async_copy(zeros, ext.at[v, pl.ds((BELOW - q) * rows, rows)], zero_sem.at[q, v])

    def zero_edge(v):
        return pltpu.make_async_copy(zeros.at[pl.ds(0, 1)], ext.at[v, pl.ds(top + rows, 1)], zero_sem.at[0, v])

    last = tile == count - 1
    upward = tile + 2 < count
    everything = range(len(pieces))

    @pl.when(upward)
    def _():
        for n in everything:
            z_copy(0, n).start()

    @pl.when(odd == 0)
    def _():
        for n in everything:
            even_copy(0, n).start()

    @pl.when(tile >= 1)
    def _():
        for n in range(2):
            edge_copy(n).start()

    for n in everything:
        core_copy(0, n).start()
    local_copy().start()

    @pl.when((tile < BELOW) | last)
    def _():
        zeros[...] = jnp.zeros_like(zeros)

    for q in range(1, BELOW + 1):

        @pl.when(tile < q)
        def _(q=q):
            for v in range(2 * views):
                zero_copy(q, v).start()

    @pl.when(last)
    def _():
        for v in range(2 * views):
            zero_edge(v).start()

    for p in range(3):
        for n in everything:

            @pl.when(tile >= 2 * p + 2)
            def _(p=p, n=n):
                z_copy(p, n).wait_recv()
                if p < 2:

                    @pl.when(upward)
                    def _():
                        z_copy(p + 1, n).start()

                    @pl.when(odd == 0)
                    def _():
                        even_copy(p + 1, n).start()

                @pl.when(odd == 1)
                def _():
                    odd_copy(p, n).start()

                core_copy(2 * p + 2, n).start()

            @pl.when(tile >= 2 * p + 1)
            def _(p=p, n=n):
                even_copy(p, n).wait_recv()
                core_copy(2 * p + 1, n).start()

    for n in everything:
        for p in range(3):

            @pl.when(upward & (tile >= 2 * p))
            def _(p=p, n=n):
                z_copy(p, n).wait_send()

            @pl.when((odd == 0) & (tile >= 2 * p))
            def _(p=p, n=n):
                even_copy(p, n).wait_send()

            @pl.when((odd == 1) & (tile >= 2 * p + 2))
            def _(p=p, n=n):
                odd_copy(p, n).wait_send()

        for q in range(BELOW + 1):

            @pl.when(tile >= q)
            def _(q=q, n=n):
                core_copy(q, n).wait()

    @pl.when(tile >= 1)
    def _():
        for n in range(2):
            edge_copy(n).wait_send()

    @pl.when(jnp.logical_not(last))
    def _():
        for n in range(2):
            pltpu.make_async_remote_copy(
                feat.at[:, pl.ds(0, 1)],
                ext.at[pl.ds((core if n == 0 else other) * views, views), pl.ds(top + rows, 1)],
                edge_send.at[n],
                edge_recv.at[n],
                device_id={"view": other},
                device_id_type=MESH,
            ).wait_recv()

    local_copy().wait()
    for q in range(1, BELOW + 1):

        @pl.when(tile < q)
        def _(q=q):
            for v in range(2 * views):
                zero_copy(q, v).wait()

    @pl.when(last)
    def _():
        for v in range(2 * views):
            zero_edge(v).wait()


def gathered(features, count):
    views, rows, channels, columns = features.shape
    n = views * PARTS
    dma = pltpu.SemaphoreType.DMA
    return pl.pallas_call(
        functools.partial(gather_kernel, count),
        out_shape=jax.ShapeDtypeStruct((2 * views, (BELOW + 1) * rows + 1, channels, columns), features.dtype),
        in_specs=[pl.BlockSpec(memory_space=pl.ANY)],
        out_specs=pl.BlockSpec(memory_space=pl.ANY),
        scratch_shapes=[
            pltpu.VMEM((rows, channels, columns), features.dtype),
            dma,
            dma((BELOW + 1, 2 * views)),
            dma((3, n)),
            dma((3, n)),
            dma((3, n)),
            dma((3, n)),
            dma((BELOW + 1, n)),
            dma((BELOW + 1, n)),
            dma((2,)),
            dma((2,)),
        ],
        compiler_params=pltpu.CompilerParams(collective_id=0, has_side_effects=True),
    )(features)


def volume_kernel(chunks, refs, marks, offs, ext, select, weight, bias, out, moved, cost, taps, ring):
    chunk = pl.program_id(0)
    half = lax.axis_index("view")
    slots = refs.shape[0]
    views, span, width, columns = ext.shape
    planes = ND // 2 + 1
    tall = 10
    own = span - tall
    sums = planes + tall - 1
    groups = width // 8
    first = own - (planes - 1) - 15 * half

    def correlate(slot, _):
        sources = [(marks[slot, v].astype(jnp.float32).astype(jnp.bfloat16), first - offs[slot, v]) for v in range(views)]
        for m in range(sums):
            rows = [ext[v, start + m] * mark for v, (mark, start) in enumerate(sources)]
            moved[pl.ds(m * width, width)] = (rows[0] + rows[1]) + (rows[2] + rows[3])
        view = refs[slot]
        for low, many in ((0, 4), (4, 4), (8, 2)):
            anchor = ext[view, pl.ds(own + low, many)].reshape(many * width, columns)
            mat = select[: many * groups, : many * width]
            for k in range(0, planes, 2):
                ks = [k, k + 1] if k + 1 < planes else [k]
                parts = [moved[pl.ds((low - kk + planes - 1) * width, many * width)] * anchor for kk in ks]
                block = jnp.concatenate(parts, axis=1) if len(parts) > 1 else parts[0]
                got = jnp.dot(mat, block, preferred_element_type=jnp.float32)
                for n, kk in enumerate(ks):
                    for row in range(many):
                        cost[slot, kk, low + row, chunk] = got[row * groups : (row + 1) * groups, n * columns : (n + 1) * columns]
        return 0

    lax.fori_loop(0, slots, correlate, 0)

    @pl.when(chunk == chunks - 1)
    def _():
        lane = lax.broadcasted_iota(jnp.int32, (chunks * groups, columns), 1)

        def regularize(slot, _):
            total = marks[slot, 0]
            for v in range(1, views):
                total = total + marks[slot, v]
            scale = 0.125 / jnp.full((chunks * groups, columns), total.astype(jnp.float32))
            taps[(planes) * half] = jnp.zeros_like(taps[0])
            spare = jnp.zeros((128 - 3 * chunks * groups, columns), jnp.float32)

            def spread(k, _):
                for row in range(tall):
                    here = cost[slot, k, row].reshape(chunks * groups, columns) * scale
                    left = jnp.where(lane == 0, 0.0, pltpu.roll(here, 1, 1))
                    right = jnp.where(lane == columns - 1, 0.0, pltpu.roll(here, columns - 1, 1))
                    block = jnp.concatenate([left, here, right, spare], axis=0)
                    taps[k + 1 - half, pl.ds(row * 128, 128)] = block.astype(jnp.bfloat16)
                return 0

            lax.fori_loop(0, planes, spread, 0)

            def convolve(plane, _):
                for row in range(0, 8, 2):
                    block = jnp.concatenate([taps[plane, pl.ds((row + n) * 128, 384)] for n in range(2)], axis=1)
                    got = jnp.dot(weight[...], block, preferred_element_type=jnp.float32)
                    for n in range(2):
                        piece = got[:, n * columns : (n + 1) * columns]
                        ring[2, row + n] = ring[1, row + n] + piece[64:]
                        ring[1, row + n] = ring[0, row + n] + piece[32:64]
                        ring[0, row + n] = piece[:32]

                @pl.when(plane >= 2)
                def _():
                    done = jnp.maximum(ring[2] + bias[...][None], 0.0)
                    out[slot, :, plane - 2] = jnp.swapaxes(done, 0, 1).astype(jnp.bfloat16)

                return 0

            lax.fori_loop(0, planes + 1, convolve, 0)
            return 0

        lax.fori_loop(0, slots, regularize, 0)


def volume(ext, refs, marks, offs, conv_weight, conv_bias):
    views, span, channels, columns = ext.shape
    slots = refs.shape[0]
    made, groups = conv_weight.shape[3], conv_weight.shape[4]
    width = 64
    chunks = channels // width
    small = width // 8
    planes = ND // 2 + 1
    weight = jnp.transpose(conv_weight, (0, 3, 1, 2, 4)).reshape(3 * made, 3, 3 * groups)
    weight = jnp.pad(weight, ((0, 0), (0, 0), (0, 128 - 3 * groups))).reshape(3 * made, 384)
    select = (jnp.arange(4 * small)[:, None] == jnp.arange(4 * width)[None, :] // 8).astype(jnp.bfloat16)
    bias = jnp.broadcast_to(conv_bias[:, None], (made, columns))
    smem = pl.BlockSpec(memory_space=pltpu.SMEM)
    shape = (slots, made, ND // 2, 8, columns)
    return pl.pallas_call(
        functools.partial(volume_kernel, chunks),
        grid=(chunks,),
        out_shape=jax.ShapeDtypeStruct(shape, jnp.bfloat16),
        in_specs=[
            smem,
            smem,
            smem,
            pl.BlockSpec((views, span, width, columns), lambda c: (0, 0, c, 0)),
            pl.BlockSpec(select.shape, lambda c: (0, 0)),
            pl.BlockSpec(weight.shape, lambda c: (0, 0)),
            pl.BlockSpec(bias.shape, lambda c: (0, 0)),
        ],
        out_specs=pl.BlockSpec(shape, lambda c: (0, 0, 0, 0, 0)),
        scratch_shapes=[
            pltpu.VMEM(((planes + 9) * width, columns), jnp.bfloat16),
            pltpu.VMEM((slots, planes, 10, chunks, small, columns), jnp.float32),
            pltpu.VMEM((planes + 1, 10 * 128, columns), jnp.bfloat16),
            pltpu.VMEM((3, 8, made, columns), jnp.float32),
        ],
        compiler_params=pltpu.CompilerParams(vmem_limit_bytes=56 * 1024 * 1024),
    )(refs, marks, offs, ext, select, weight, bias)


def shards(count, features, ref_views, intersection, offsets, conv_weight, conv_bias):
    ext = gathered(features, count)
    return volume(ext, ref_views, intersection, offsets, conv_weight, conv_bias)


def solution(mesh):
    placed = (
        P(("groups", "view"), "tile", None, None),
        P("groups"),
        P("groups", None),
        P("groups", None),
        P(),
        P(),
    )
    return jax.shard_map(
        functools.partial(shards, mesh.shape["tile"]),
        mesh=mesh,
        in_specs=placed,
        out_specs=P("groups", None, "view", "tile", None),
        check_vma=False,
    )
```

time: 648 us -> 156 us (0.24); the launches traced: 640 us -> 156 us
  other arithmetic: 251 us -> 0.61 us
  waiting for transfers between devices: 173 us -> 0 us
  Pallas kernels: 0 us -> 152 us
  starting transfers between devices: 61.9 us -> 0 us
  matrix products: 61 us -> 0 us
  local copies, waits for them, and re-layouts: 49.8 us -> 3.3 us
  between operations: 43.6 us -> 0.03 us
    pallas_call x0 -> x2, Pallas kernels: none -> 152 us  [the longest x1 99.7 us: gathered(): pl.pallas_call(functools.partial(gather_kernel, count), out_shape=jax.Sha...]
    reduce_sum x17 -> x0, other arithmetic: 134 us -> none  [the longest x16 133 us: group_products(): jnp.sum(product.reshape(rows, groups, channels // groups, columns), axis=2)]
    ppermute x22 -> x0, waiting for transfers between devices: 131 us -> none  [the longest x6 131 us: passed_along(): lax.ppermute(value, axis, [(source, source + steps) for source in range(f...]
    unnamed x268 -> x0, other arithmetic: 76.7 us -> none
    ppermute x22 -> x0, starting transfers between devices: 61.8 us -> none  [the longest x8 30.9 us: padded_2(): lax.ppermute(head, axis, [((i + 1) % count, i) for i in range(ends)])]
    dot_general x12 -> x0, matrix products: 61 us -> none  [regularize(): jnp.einsum('ok,kdrw->odrw', tap_matrix, stacked[:, depth_tap:depth_tap +...]
    reduce_scatter x4 -> x0, waiting for transfers between devices: 41.2 us -> none  [shards(): lax.psum_scatter(partial_value.astype(jnp.bfloat16), 'view', scatter_dime...]
    unnamed x208 -> x3, local copies, waits for them, and re-layouts: 33.4 us -> 1.92 us
  transfers between devices with their start and end apart: 27 -> 0, of which waited for: 5 -> 0; matrix products, arithmetic and copies ran while one was open for 42% -> 0% of each run, Pallas kernels for 0% -> 0%
where the time goes in v1:
time: 156 us
  Pallas kernels  152 us (97%)
  local copies, waits for them, and re-layouts  3.3 us (2%)
    pallas_call x1, Pallas kernels, gathered(): pl.pallas_call(functools.partial(gather_kernel, count), out_shape=jax.Sha...  99.7 us
    pallas_call x1, Pallas kernels, volume(): pl.pallas_call(functools.partial(volume_kernel, chunks), grid=(chunks,),...  52.1 us

profile of v1, /device:TPU:24, one launch (start us, length us, event | category | flops | bytes accessed | tf_op | source)
XLA Modules:
  0.0 155.7 jit_solution(15817091580736308931)
XLA Ops:
  0.0 0.6 fusion.select
  0.6 1.3 broadcast_in_dim.2.bias
  1.9 1.1 copy.10
  3.0 0.2 reshape.46
  3.2 0.1 pad.4.clone
  3.3 0.6 copy.14
  3.9 99.7 %shard_map.64.ext = bf16[4,57,320,128]{3,2,1,0:T(8,128)(2,1)} custom-call(bf16[2,8,320,128]{3,2,1,0:T(8,128)(2,1)} %feat.1), custom_call_target="tpu_custom_call" | custom-call | tf_op jit(solution)/shard_map/pallas_call | solution.py:207
  103.6 52.1 %shard_map.65 = bf16[4,32,16,8,128]{4,3,2,1,0:T(8,128)(2,1)} custom-call(s32[4]{0:T(128)} %refs.1, s32[4,4]{1,0:T(4,128)} %marks.1, s32[4,4]{1,0:T(4,128)} %offs.1, bf16[4,57,320,128]{3,2,1,0:T(8,128)(2,1)} %shard_map.64.ext, bf16[32,256]{1,0:T(8,128)(2,1)} %fusion.select, bf16[96,384]{1,0:T(8,128)(2,1)} %bitcast.6, f32[32,128]{1,0:T(8,128)} %broadcast_in_dim.2.bias), custom_call_target="tpu_custom_call" | custom-call | tf_op jit(solution)/shard_map/pallas_call | solution.py:322
  (1 shorter events, 0.0 us)

commit v2 on v1

v2 whole, which is shorter than its diff:
```python
import functools

import jax
import jax.numpy as jnp
from jax import lax
from jax.experimental import pallas as pl
from jax.experimental.pallas import tpu as pltpu
from jax.sharding import PartitionSpec as P

ND = 32
OFF = 17
BELOW = 6
MESH = pl.DeviceIdType.MESH
WIDTH = 64


def gather_kernel(count, feat, refs, marks, offs, select, out, *scratch):
    views, rows, channels, columns = feat.shape
    parts = channels // WIDTH
    ext, rest = scratch[:parts], scratch[parts:]
    moved, cost, local_sem, out_sem, z_send, z_recv, pair_send, pair_recv, core_send, core_recv, edge_send, edge_recv = rest
    tile = lax.axis_index("tile")
    core = lax.axis_index("view")
    other = 1 - core
    odd = tile % 2
    partner = tile + 1 - 2 * odd
    top = BELOW * rows

    barrier = pltpu.get_barrier_semaphore()
    pl.semaphore_signal(barrier, inc=1, device_id={"view": other}, device_id_type=MESH)
    peers = jnp.int32(1)
    for shift, both in ((2, False), (-2, False), (1, True), (-1, True)):
        there = (tile + shift >= 0) & (tile + shift < count)
        peers = peers + jnp.where(there, 2 if both else 1, 0)

        @pl.when(there)
        def _(shift=shift, both=both):
            pl.semaphore_signal(barrier, inc=1, device_id={"tile": tile + shift}, device_id_type=MESH)
            if both:
                pl.semaphore_signal(barrier, inc=1, device_id={"tile": tile + shift, "view": other}, device_id_type=MESH)

    pl.semaphore_wait(barrier, peers)

    def slot(q, n):
        return ext[n].at[pl.ds(core * views, views), pl.ds((BELOW - q) * rows, rows)]

    def mine(n):
        return feat.at[:, :, pl.ds(n * WIDTH, WIDTH)]

    def z_copy(p, n):
        src = mine(n) if p == 0 else slot(2 * p, n)
        return pltpu.make_async_remote_copy(src, slot(2 * p + 2, n), z_send.at[p, n], z_recv.at[p, n], device_id={"tile": tile + 2}, device_id_type=MESH)

    def even_copy(k, n):
        src = mine(n) if k == 0 else slot(2 * k, n)
        return pltpu.make_async_remote_copy(src, slot(2 * k + 1, n), pair_send.at[k, n], pair_recv.at[k, n], device_id={"tile": partner}, device_id_type=MESH)

    def odd_copy(k, n):
        return pltpu.make_async_remote_copy(slot(2 * k + 2, n), slot(2 * k + 1, n), pair_send.at[k, n], pair_recv.at[k, n], device_id={"tile": partner}, device_id_type=MESH)

    def core_copy(q, n):
        src = mine(n) if q == 0 else slot(q, n)
        return pltpu.make_async_remote_copy(src, slot(q, n), core_send.at[q, n], core_recv.at[q, n], device_id={"view": other}, device_id_type=MESH)

    def edge_copy(n, far, side):
        return pltpu.make_async_remote_copy(
            feat.at[:, pl.ds(0, 1), pl.ds(n * WIDTH, WIDTH)],
            ext[n].at[pl.ds(side * views, views), pl.ds(top + rows, 1)],
            edge_send.at[far, n],
            edge_recv.at[far, n],
            device_id={"tile": tile - 1, "view": other if far else core},
            device_id_type=MESH,
        )

    def local_copy(n):
        return pltpu.make_async_copy(mine(n), slot(0, n), local_sem.at[n])

    def out_copy(n):
        return pltpu.make_async_copy(cost.at[n], out.at[n], out_sem.at[n])

    def blank(low, many):
        for n in everything:
            for v in range(2 * views):
                ext[n][v, low : low + many] = jnp.zeros((many, WIDTH, columns), feat.dtype)

    last = tile == count - 1
    upward = tile + 2 < count
    everything = range(parts)

    @pl.when(upward)
    def _():
        for n in everything:
            z_copy(0, n).start()

    @pl.when(odd == 0)
    def _():
        for n in everything:
            even_copy(0, n).start()

    for n in everything:
        local_copy(n).start()
        core_copy(0, n).start()

    @pl.when(tile >= 1)
    def _():
        for n in everything:
            for far in range(2):
                edge_copy(n, far, core).start()

    for q in range(1, BELOW + 1):

        @pl.when(tile < q)
        def _(q=q):
            blank((BELOW - q) * rows, rows)

    @pl.when(last)
    def _():
        blank(top + rows, 1)

    def compute(n):
        for q in range(BELOW + 1):

            @pl.when(tile >= q)
            def _(q=q):
                core_copy(q, n).wait_recv()

        @pl.when(jnp.logical_not(last))
        def _():
            for far in range(2):
                edge_copy(n, far, other if far else core).wait_recv()

        local_copy(n).wait()
        correlate(ext[n], refs, marks, offs, select, moved, cost.at[n], core)
        out_copy(n).start()

    for p in range(3):
        for n in everything:

            @pl.when(tile >= 2 * p + 2)
            def _(p=p, n=n):
                z_copy(p, n).wait_recv()
                if p < 2:

                    @pl.when(upward)
                    def _():
                        z_copy(p + 1, n).start()

                    @pl.when(odd == 0)
                    def _():
                        even_copy(p + 1, n).start()

                @pl.when(odd == 1)
                def _():
                    odd_copy(p, n).start()

                core_copy(2 * p + 2, n).start()

            @pl.when(tile >= 2 * p + 1)
            def _(p=p, n=n):
                even_copy(p, n).wait_recv()
                core_copy(2 * p + 1, n).start()

            if p == 2 and n > 0:
                compute(n - 1)

    compute(parts - 1)

    for n in everything:
        for p in range(3):

            @pl.when(upward & (tile >= 2 * p))
            def _(p=p, n=n):
                z_copy(p, n).wait_send()

            @pl.when((odd == 0) & (tile >= 2 * p))
            def _(p=p, n=n):
                even_copy(p, n).wait_send()

            @pl.when((odd == 1) & (tile >= 2 * p + 2))
            def _(p=p, n=n):
                odd_copy(p, n).wait_send()

        for q in range(BELOW + 1):

            @pl.when(tile >= q)
            def _(q=q, n=n):
                core_copy(q, n).wait_send()

        @pl.when(tile >= 1)
        def _(n=n):
            for far in range(2):
                edge_copy(n, far, core).wait_send()

        out_copy(n).wait()


def correlate(ext, refs, marks, offs, select, moved, cost, half):
    slots = refs.shape[0]
    views, span, width, columns = ext.shape
    planes = ND // 2 + 1
    tall = 10
    own = span - tall
    sums = planes + tall - 1
    first = own - (planes - 1) - 15 * half

    def one(slot, _):
        sources = [(marks[slot, v].astype(jnp.float32).astype(jnp.bfloat16), first - offs[slot, v]) for v in range(views)]
        total = marks[slot, 0]
        for v in range(1, views):
            total = total + marks[slot, v]
        scale = 0.125 / jnp.full((8, columns), total.astype(jnp.float32))
        for m in range(sums):
            rows = [ext[v, start + m] * mark for v, (mark, start) in enumerate(sources)]
            moved[m * width : (m + 1) * width] = (rows[0] + rows[1]) + (rows[2] + rows[3])
        view = refs[slot]
        for low, many in ((0, 4), (4, 4), (8, 2)):
            anchor = ext[view, own + low : own + low + many].reshape(many * width, columns)
            mat = select[: many * 8, : many * width]
            factor = jnp.concatenate([scale] * many, axis=0)
            for k in range(0, planes, 2):
                ks = [k, k + 1] if k + 1 < planes else [k]
                blocks = []
                for kk in ks:
                    at = (low - kk + planes - 1) * width
                    blocks.append(moved[at : at + many * width] * anchor)
                block = jnp.concatenate(blocks, axis=1) if len(blocks) > 1 else blocks[0]
                got = jnp.dot(mat, block, preferred_element_type=jnp.float32)
                for n, kk in enumerate(ks):
                    cost[slot, kk, low * 8 : (low + many) * 8] = (got[:, n * columns : (n + 1) * columns] * factor).astype(jnp.bfloat16)
        return 0

    lax.fori_loop(0, slots, one, 0)


def gathered(features, refs, marks, offs, count):
    views, rows, channels, columns = features.shape
    slots = refs.shape[0]
    n = channels // WIDTH
    planes = ND // 2 + 1
    span = (BELOW + 1) * rows + 1
    select = (jnp.arange(32)[:, None] == jnp.arange(4 * WIDTH)[None, :] // 8).astype(jnp.bfloat16)
    dma = pltpu.SemaphoreType.DMA
    shape = (n, slots, planes, 80, columns)
    smem = pl.BlockSpec(memory_space=pltpu.SMEM)
    return pl.pallas_call(
        functools.partial(gather_kernel, count),
        out_shape=jax.ShapeDtypeStruct(shape, features.dtype),
        in_specs=[pl.BlockSpec(memory_space=pl.ANY), smem, smem, smem, pl.BlockSpec(memory_space=pltpu.VMEM)],
        out_specs=pl.BlockSpec(memory_space=pl.ANY),
        scratch_shapes=[pltpu.VMEM((2 * views, span, WIDTH, columns), features.dtype) for _ in range(n)]
        + [
            pltpu.VMEM(((planes + 9) * WIDTH, columns), features.dtype),
            pltpu.VMEM(shape, features.dtype),
            dma((n,)),
            dma((n,)),
            dma((3, n)),
            dma((3, n)),
            dma((3, n)),
            dma((3, n)),
            dma((BELOW + 1, n)),
            dma((BELOW + 1, n)),
            dma((2, n)),
            dma((2, n)),
        ],
        compiler_params=pltpu.CompilerParams(collective_id=0, has_side_effects=True, vmem_limit_bytes=48 * 1024 * 1024),
    )(features, refs, marks, offs, select)


def volume_kernel(cost, weight, bias, out, taps, ring):
    half = lax.axis_index("view")
    parts, planes, columns = cost.shape[0], cost.shape[2], cost.shape[4]
    tall = 10
    groups = parts * 8
    lane = lax.broadcasted_iota(jnp.int32, (groups, columns), 1)
    spare = jnp.zeros((128 - 3 * groups, columns), jnp.float32)
    taps[planes * half] = jnp.zeros_like(taps[0])

    def spread(k, _):
        for pair in range(0, tall, 2):
            both = [cost[n, 0, k, pair * 8 : pair * 8 + 16].astype(jnp.float32) for n in range(parts)]
            for row in range(2):
                here = jnp.concatenate([one[row * 8 : row * 8 + 8] for one in both], axis=0)
                left = jnp.where(lane == 0, 0.0, pltpu.roll(here, 1, 1))
                right = jnp.where(lane == columns - 1, 0.0, pltpu.roll(here, columns - 1, 1))
                block = jnp.concatenate([left, here, right, spare], axis=0)
                taps[k + 1 - half, (pair + row) * 128 : (pair + row + 1) * 128] = block.astype(jnp.bfloat16)
        return 0

    lax.fori_loop(0, planes, spread, 0)

    def convolve(plane, _):
        for row in range(0, 8, 2):
            block = jnp.concatenate([taps[plane, (row + n) * 128 : (row + n + 3) * 128] for n in range(2)], axis=1)
            got = jnp.dot(weight[...], block, preferred_element_type=jnp.float32)
            for n in range(2):
                piece = got[:, n * columns : (n + 1) * columns]
                ring[2, row + n] = ring[1, row + n] + piece[64:]
                ring[1, row + n] = ring[0, row + n] + piece[32:64]
                ring[0, row + n] = piece[:32]

        @pl.when(plane >= 2)
        def _():
            done = jnp.maximum(ring[2] + bias[...][None], 0.0)
            out[0, :, plane - 2] = jnp.swapaxes(done, 0, 1).astype(jnp.bfloat16)

        return 0

    lax.fori_loop(0, planes + 1, convolve, 0)


def volume(cost, conv_weight, conv_bias):
    parts, slots, planes, tall, columns = cost.shape
    made, groups = conv_weight.shape[3], conv_weight.shape[4]
    weight = jnp.transpose(conv_weight, (0, 3, 1, 2, 4)).reshape(3 * made, 3, 3 * groups)
    weight = jnp.pad(weight, ((0, 0), (0, 0), (0, 128 - 3 * groups))).reshape(3 * made, 384)
    bias = jnp.broadcast_to(conv_bias[:, None], (made, columns))
    shape = (slots, made, ND // 2, 8, columns)
    return pl.pallas_call(
        volume_kernel,
        grid=(slots,),
        out_shape=jax.ShapeDtypeStruct(shape, jnp.bfloat16),
        in_specs=[
            pl.BlockSpec((parts, 1, planes, tall, columns), lambda r: (0, r, 0, 0, 0)),
            pl.BlockSpec(weight.shape, lambda r: (0, 0)),
            pl.BlockSpec(bias.shape, lambda r: (0, 0)),
        ],
        out_specs=pl.BlockSpec((1,) + shape[1:], lambda r: (r, 0, 0, 0, 0)),
        scratch_shapes=[
            pltpu.VMEM((planes + 1, 10 * 128, columns), jnp.bfloat16),
            pltpu.VMEM((3, 8, made, columns), jnp.float32),
        ],
        compiler_params=pltpu.CompilerParams(vmem_limit_bytes=32 * 1024 * 1024),
    )(cost, weight, bias)


def shards(count, features, ref_views, intersection, offsets, conv_weight, conv_bias):
    cost = gathered(features, ref_views, intersection, offsets, count)
    return volume(cost, conv_weight, conv_bias)


def solution(mesh):
    placed = (
        P(("groups", "view"), "tile", None, None),
        P("groups"),
        P("groups", None),
        P("groups", None),
        P(),
        P(),
    )
    return jax.shard_map(
        functools.partial(shards, mesh.shape["tile"]),
        mesh=mesh,
        in_specs=placed,
        out_specs=P("groups", None, "view", "tile", None),
        check_vma=False,
    )
```

time: 156 us -> 147 us (0.942)
  Pallas kernels: 152 us -> 138 us
  local copies, waits for them, and re-layouts: 3.3 us -> 8.37 us
    pallas_call x1, Pallas kernels: 52.1 us -> 33.6 us  [volume(): pl.pallas_call(volume_kernel, grid=(slots,), out_shape=jax.ShapeDtypeStru...]
    unnamed x3 -> x13, local copies, waits for them, and re-layouts: 1.92 us -> 7.59 us
    pallas_call x1, Pallas kernels: 99.7 us -> 104 us  [gathered(): pl.pallas_call(functools.partial(gather_kernel, count), out_shape=jax.Sha...]
where the time goes in v2:
time: 147 us; the launch traced here: 146 us
  Pallas kernels  138 us (94%)
  local copies, waits for them, and re-layouts  8.37 us (6%)
    pallas_call x1, Pallas kernels, gathered(): pl.pallas_call(functools.partial(gather_kernel, count), out_shape=jax.Sha...  104 us
    pallas_call x1, Pallas kernels, volume(): pl.pallas_call(volume_kernel, grid=(slots,), out_shape=jax.ShapeDtypeStru...  33.6 us
    unnamed x13, local copies, waits for them, and re-layouts  7.59 us

profile of v2, /device:TPU:24, one launch (start us, length us, event | category | flops | bytes accessed | tf_op | source)
XLA Modules:
  0.0 146.5 jit_solution(887406059250438141)
XLA Ops:
  0.0 0.7 broadcast_in_dim.2.bias
  0.7 1.1 copy.10
  1.8 0.2 reshape.46
  2.0 0.1 pad.4.clone
  2.1 0.0 copy-start.1
  2.1 1.3 copy-done.1
  3.4 0.0 copy-start.2
  3.4 0.7 copy-done.2
  4.1 0.0 copy-start.3
  4.1 0.7 copy-done.3
  4.8 0.0 copy-start.4
  4.8 0.7 copy-done.4
  5.4 104.5 %shard_map.64.cost = bf16[5,4,17,80,128]{4,3,2,1,0:T(8,128)(2,1)} custom-call(bf16[2,8,320,128]{3,2,1,0:T(8,128)(2,1)S(1)} %copy-done.1, s32[4]{0:T(128)S(1)} %copy-done.4, s32[4,4]{1,0:T(4,128)S(1)} %copy-done.2, s32[4,4]{1,0:T(4,128)S(1)} %copy-done.3, bf16[32,256]{1,0:T(8,128)(2,1)S(1)} %fusion.select), custom_call_target="tpu_custom_call" | custom-call | tf_op jit(solution)/shard_map/pallas_call | solution.py:245
  109.9 0.0 copy-start
  109.9 3.0 %copy-done = bf16[5,4,17,80,128]{4,3,2,1,0:T(8,128)(2,1)S(1)} copy-done((bf16[5,4,17,80,128]{4,3,2,1,0:T(8,128)(2,1)S(1)}, bf16[5,4,17,80,128]{4,3,2,1,0:T(8,128)(2,1)}, u32[]{:S(2)}) %copy-start) | copy-done | bytes 6963224
  112.9 33.6 %shard_map.65 = bf16[4,32,16,8,128]{4,3,2,1,0:T(8,128)(2,1)} custom-call(bf16[5,4,17,80,128]{4,3,2,1,0:T(8,128)(2,1)S(1)} %copy-done, bf16[96,384]{1,0:T(8,128)(2,1)S(1)} %bitcast.5, f32[32,128]{1,0:T(8,128)S(1)} %broadcast_in_dim.2.bias), custom_call_target="tpu_custom_call" | custom-call | tf_op jit(solution)/shard_map/pallas_call | solution.py:318
  (3 shorter events, 0.0 us)
Async XLA Ops:
  2.1 1.3 copy-start.1
  3.4 0.7 copy-start.2
  4.1 0.7 copy-start.3
  4.8 0.7 copy-start.4
  109.9 3.0 %copy-start = (bf16[5,4,17,80,128]{4,3,2,1,0:T(8,128)(2,1)S(1)}, bf16[5,4,17,80,128]{4,3,2,1,0:T(8,128)(2,1)}, u32[]{:S(2)}) copy-start(bf16[5,4,17,80,128]{4,3,2,1,0:T(8,128)(2,1)} %shard_map.64.cost) | copy-start | bytes 20889604

commit v3 on v2

--- a/solution.py
+++ b/solution.py
@@ -262,7 +262,7 @@
             dma((2, n)),
             dma((2, n)),
         ],
-        compiler_params=pltpu.CompilerParams(collective_id=0, has_side_effects=True, vmem_limit_bytes=48 * 1024 * 1024),
+        compiler_params=pltpu.CompilerParams(collective_id=0, has_side_effects=True, vmem_limit_bytes=60 * 1024 * 1024),
     )(features, refs, marks, offs, select)
 
 
@@ -275,7 +275,7 @@
     spare = jnp.zeros((128 - 3 * groups, columns), jnp.float32)
     taps[planes * half] = jnp.zeros_like(taps[0])
 
-    def spread(k, _):
+    def spread(k):
         for pair in range(0, tall, 2):
             both = [cost[n, 0, k, pair * 8 : pair * 8 + 16].astype(jnp.float32) for n in range(parts)]
             for row in range(2):
@@ -284,28 +284,29 @@
                 right = jnp.where(lane == columns - 1, 0.0, pltpu.roll(here, columns - 1, 1))
                 block = jnp.concatenate([left, here, right, spare], axis=0)
                 taps[k + 1 - half, (pair + row) * 128 : (pair + row + 1) * 128] = block.astype(jnp.bfloat16)
-        return 0
-
-    lax.fori_loop(0, planes, spread, 0)
-
-    def convolve(plane, _):
-        for row in range(0, 8, 2):
-            block = jnp.concatenate([taps[plane, (row + n) * 128 : (row + n + 3) * 128] for n in range(2)], axis=1)
+
+    for k in range(planes):
+        spread(k)
+
+    def convolve(plane):
+        for row in range(0, 8, 4):
+            block = jnp.concatenate([taps[plane, (row + n) * 128 : (row + n + 4) * 128] for n in (0, 2)], axis=1)
             got = jnp.dot(weight[...], block, preferred_element_type=jnp.float32)
-            for n in range(2):
-                piece = got[:, n * columns : (n + 1) * columns]
+            for n in range(4):
+                low = (n % 2) * 96
+                piece = got[low : low + 96, (n // 2) * columns : (n // 2 + 1) * columns]
                 ring[2, row + n] = ring[1, row + n] + piece[64:]
                 ring[1, row + n] = ring[0, row + n] + piece[32:64]
                 ring[0, row + n] = piece[:32]
 
-        @pl.when(plane >= 2)
-        def _():
-            done = jnp.maximum(ring[2] + bias[...][None], 0.0)
-            out[0, :, plane - 2] = jnp.swapaxes(done, 0, 1).astype(jnp.bfloat16)
-
-        return 0
-
-    lax.fori_loop(0, planes + 1, convolve, 0)
+    def finish(plane):
+        done = jnp.maximum(ring[2] + bias[...][None], 0.0)
+        out[0, :, plane - 2] = jnp.swapaxes(done, 0, 1).astype(jnp.bfloat16)
+
+    for plane in range(planes + 1):
+        convolve(plane)
+        if plane >= 2:
+            finish(plane)
 
 
 def volume(cost, conv_weight, conv_bias):
@@ -313,6 +314,7 @@
     made, groups = conv_weight.shape[3], conv_weight.shape[4]
     weight = jnp.transpose(conv_weight, (0, 3, 1, 2, 4)).reshape(3 * made, 3, 3 * groups)
     weight = jnp.pad(weight, ((0, 0), (0, 0), (0, 128 - 3 * groups))).reshape(3 * made, 384)
+    weight = jnp.concatenate([jnp.pad(weight, ((0, 0), (128 * n, 128 - 128 * n))) for n in range(2)], axis=0)
     bias = jnp.broadcast_to(conv_bias[:, None], (made, columns))
     shape = (slots, made, ND // 2, 8, columns)
     return pl.pallas_call(
@@ -329,7 +331,7 @@
             pltpu.VMEM((planes + 1, 10 * 128, columns), jnp.bfloat16),
             pltpu.VMEM((3, 8, made, columns), jnp.float32),
         ],
-        compiler_params=pltpu.CompilerParams(vmem_limit_bytes=32 * 1024 * 1024),
+        compiler_params=pltpu.CompilerParams(vmem_limit_bytes=60 * 1024 * 1024),
     )(cost, weight, bias)
 
 

time: 147 us -> 129 us (0.88)
  Pallas kernels: 138 us -> 125 us
  local copies, waits for them, and re-layouts: 8.37 us -> 2.67 us
    pallas_call x1, Pallas kernels: 33.6 us -> 20.2 us  [volume(): pl.pallas_call(volume_kernel, grid=(slots,), out_shape=jax.ShapeDtypeStru...]
    unnamed x13 -> x3, local copies, waits for them, and re-layouts: 7.59 us -> 1.29 us
where the time goes in v3:
time: 129 us
  Pallas kernels  125 us (97%)
  local copies, waits for them, and re-layouts  2.67 us (2%)
  other arithmetic  1.31 us (1%)
    pallas_call x1, Pallas kernels, gathered(): pl.pallas_call(functools.partial(gather_kernel, count), out_shape=jax.Sha...  105 us
    pallas_call x1, Pallas kernels, volume(): pl.pallas_call(volume_kernel, grid=(slots,), out_shape=jax.ShapeDtypeStru...  20.2 us

profile of v3, /device:TPU:24, one launch (start us, length us, event | category | flops | bytes accessed | tf_op | source)
XLA Modules:
  0.0 129.0 jit_solution(14963752834182895833)
XLA Ops:
  0.0 0.6 fusion.3.select
  0.6 1.3 %broadcast_in_dim.2.bias = f32[32,128]{1,0:T(8,128)} broadcast(f32[32]{0:T(128)} %param.11), dimensions={0} | broadcast | bytes 16512 | tf_op jit(solution)/shard_map/broadcast_in_dim | solution.py:318
  1.9 1.1 copy.10
  3.0 0.2 reshape.46
  3.2 0.1 pad.12.clone
  3.3 0.7 fusion.2.weight
  4.0 104.8 %shard_map.64.cost = bf16[5,4,17,80,128]{4,3,2,1,0:T(8,128)(2,1)} custom-call(bf16[2,8,320,128]{3,2,1,0:T(8,128)(2,1)} %feat.1, s32[4]{0:T(128)} %refs.1, s32[4,4]{1,0:T(4,128)} %marks.1, s32[4,4]{1,0:T(4,128)} %offs.1, bf16[32,256]{1,0:T(8,128)(2,1)} %fusion.3.select), custom_call_target="tpu_custom_call" | custom-call | tf_op jit(solution)/shard_map/pallas_call | solution.py:245
  108.8 20.2 %shard_map.65 = bf16[4,32,16,8,128]{4,3,2,1,0:T(8,128)(2,1)} custom-call(bf16[5,4,17,80,128]{4,3,2,1,0:T(8,128)(2,1)} %shard_map.64.cost, bf16[192,512]{1,0:T(8,128)(2,1)} %fusion.2.weight, f32[32,128]{1,0:T(8,128)} %broadcast_in_dim.2.bias), custom_call_target="tpu_custom_call" | custom-call | tf_op jit(solution)/shard_map/pallas_call | solution.py:320
  (2 shorter events, 0.0 us)

commit v4 on v3

--- a/solution.py
+++ b/solution.py
@@ -14,11 +14,11 @@
 WIDTH = 64
 
 
-def gather_kernel(count, feat, refs, marks, offs, select, out, *scratch):
+def gather_kernel(count, feat, refs, marks, offs, out, *scratch):
     views, rows, channels, columns = feat.shape
     parts = channels // WIDTH
     ext, rest = scratch[:parts], scratch[parts:]
-    moved, cost, local_sem, out_sem, z_send, z_recv, pair_send, pair_recv, core_send, core_recv, edge_send, edge_recv = rest
+    select, moved, cost, local_sem, out_sem, z_send, z_recv, pair_send, pair_recv, core_send, core_recv, edge_send, edge_recv = rest
     tile = lax.axis_index("tile")
     core = lax.axis_index("view")
     other = 1 - core
@@ -107,6 +107,11 @@
             for far in range(2):
                 edge_copy(n, far, core).start()
 
+    group = lax.broadcasted_iota(jnp.int32, select.shape, 0)
+    channel = lax.broadcasted_iota(jnp.int32, select.shape, 1)
+    member = (channel >= group * 8) & (channel < group * 8 + 8)
+    select[...] = jnp.where(member, 1.0, 0.0).astype(select.dtype)
+
     for q in range(1, BELOW + 1):
 
         @pl.when(tile < q)
@@ -133,6 +138,12 @@
         correlate(ext[n], refs, marks, offs, select, moved, cost.at[n], core)
         out_copy(n).start()
 
+    def paired(p, n):
+        @pl.when(tile >= 2 * p + 1)
+        def _():
+            even_copy(p, n).wait_recv()
+            core_copy(2 * p + 1, n).start()
+
     for p in range(3):
         for n in everything:
 
@@ -155,14 +166,13 @@
 
                 core_copy(2 * p + 2, n).start()
 
-            @pl.when(tile >= 2 * p + 1)
-            def _(p=p, n=n):
-                even_copy(p, n).wait_recv()
-                core_copy(2 * p + 1, n).start()
+            if p + n > 0:
+                paired(*((p, n - 1) if n > 0 else (p - 1, parts - 1)))
 
             if p == 2 and n > 0:
                 compute(n - 1)
 
+    paired(2, parts - 1)
     compute(parts - 1)
 
     for n in everything:
@@ -238,17 +248,17 @@
     n = channels // WIDTH
     planes = ND // 2 + 1
     span = (BELOW + 1) * rows + 1
-    select = (jnp.arange(32)[:, None] == jnp.arange(4 * WIDTH)[None, :] // 8).astype(jnp.bfloat16)
     dma = pltpu.SemaphoreType.DMA
     shape = (n, slots, planes, 80, columns)
     smem = pl.BlockSpec(memory_space=pltpu.SMEM)
     return pl.pallas_call(
         functools.partial(gather_kernel, count),
         out_shape=jax.ShapeDtypeStruct(shape, features.dtype),
-        in_specs=[pl.BlockSpec(memory_space=pl.ANY), smem, smem, smem, pl.BlockSpec(memory_space=pltpu.VMEM)],
+        in_specs=[pl.BlockSpec(memory_space=pl.ANY), smem, smem, smem],
         out_specs=pl.BlockSpec(memory_space=pl.ANY),
         scratch_shapes=[pltpu.VMEM((2 * views, span, WIDTH, columns), features.dtype) for _ in range(n)]
         + [
+            pltpu.VMEM((32, 4 * WIDTH), features.dtype),
             pltpu.VMEM(((planes + 9) * WIDTH, columns), features.dtype),
             pltpu.VMEM(shape, features.dtype),
             dma((n,)),
@@ -263,10 +273,12 @@
             dma((2, n)),
         ],
         compiler_params=pltpu.CompilerParams(collective_id=0, has_side_effects=True, vmem_limit_bytes=60 * 1024 * 1024),
-    )(features, refs, marks, offs, select)
-
-
-def volume_kernel(cost, weight, bias, out, taps, ring):
+    )(features, refs, marks, offs)
+
+
+def volume_kernel(cost, weight, shift, out, taps, ring, bias):
+    for o in range(bias.shape[0]):
+        bias[o : o + 1] = jnp.full((1, bias.shape[1]), shift[o])
     half = lax.axis_index("view")
     parts, planes, columns = cost.shape[0], cost.shape[2], cost.shape[4]
     tall = 10
@@ -315,7 +327,6 @@
     weight = jnp.transpose(conv_weight, (0, 3, 1, 2, 4)).reshape(3 * made, 3, 3 * groups)
     weight = jnp.pad(weight, ((0, 0), (0, 0), (0, 128 - 3 * groups))).reshape(3 * made, 384)
     weight = jnp.concatenate([jnp.pad(weight, ((0, 0), (128 * n, 128 - 128 * n))) for n in range(2)], axis=0)
-    bias = jnp.broadcast_to(conv_bias[:, None], (made, columns))
     shape = (slots, made, ND // 2, 8, columns)
     return pl.pallas_call(
         volume_kernel,
@@ -324,15 +335,16 @@
         in_specs=[
             pl.BlockSpec((parts, 1, planes, tall, columns), lambda r: (0, r, 0, 0, 0)),
             pl.BlockSpec(weight.shape, lambda r: (0, 0)),
-            pl.BlockSpec(bias.shape, lambda r: (0, 0)),
+            pl.BlockSpec(memory_space=pltpu.SMEM),
         ],
         out_specs=pl.BlockSpec((1,) + shape[1:], lambda r: (r, 0, 0, 0, 0)),
         scratch_shapes=[
             pltpu.VMEM((planes + 1, 10 * 128, columns), jnp.bfloat16),
             pltpu.VMEM((3, 8, made, columns), jnp.float32),
+            pltpu.VMEM((made, columns), jnp.float32),
         ],
         compiler_params=pltpu.CompilerParams(vmem_limit_bytes=60 * 1024 * 1024),
-    )(cost, weight, bias)
+    )(cost, weight, conv_bias)
 
 
 def shards(count, features, ref_views, intersection, offsets, conv_weight, conv_bias):

time: 129 us -> 126 us (0.977); the launches traced: 129 us -> 124 us
  Pallas kernels: 125 us -> 122 us
  local copies, waits for them, and re-layouts: 2.67 us -> 1.34 us
    pallas_call x1, Pallas kernels: 105 us -> 102 us  [gathered(): pl.pallas_call(functools.partial(gather_kernel, count), out_shape=jax.Sha...]
    broadcast_in_dim x1 -> x0, local copies, waits for them, and re-layouts: 1.32 us -> none  [volume(): bias = jnp.broadcast_to(conv_bias[:, None], (made, columns))]
where the time goes in v4:
time: 126 us; the launch traced here: 124 us
  Pallas kernels  122 us (97%)
  local copies, waits for them, and re-layouts  1.34 us (1%)
    pallas_call x1, Pallas kernels, gathered(): pl.pallas_call(functools.partial(gather_kernel, count), out_shape=jax.Sha...  102 us
    pallas_call x1, Pallas kernels, volume(): pl.pallas_call(volume_kernel, grid=(slots,), out_shape=jax.ShapeDtypeStru...  19.7 us

profile of v4, /device:TPU:24, one launch (start us, length us, event | category | flops | bytes accessed | tf_op | source)
XLA Modules:
  0.0 124.2 jit_solution(9365129589314011762)
XLA Ops:
  0.0 1.1 copy.10
  1.1 0.2 reshape.8
  1.3 0.1 pad.12.clone
  1.4 0.7 fusion.2.weight
  2.1 102.4 %shard_map.64.cost = bf16[5,4,17,80,128]{4,3,2,1,0:T(8,128)(2,1)} custom-call(bf16[2,8,320,128]{3,2,1,0:T(8,128)(2,1)} %feat.1, s32[4]{0:T(128)} %refs.1, s32[4,4]{1,0:T(4,128)} %marks.1, s32[4,4]{1,0:T(4,128)} %offs.1), custom_call_target="tpu_custom_call" | custom-call | tf_op jit(solution)/shard_map/pallas_call | solution.py:254
  104.5 19.7 %shard_map.65 = bf16[4,32,16,8,128]{4,3,2,1,0:T(8,128)(2,1)} custom-call(bf16[5,4,17,80,128]{4,3,2,1,0:T(8,128)(2,1)} %shard_map.64.cost, bf16[192,512]{1,0:T(8,128)(2,1)} %fusion.2.weight, f32[32]{0:T(128)} %shift.1), custom_call_target="tpu_custom_call" | custom-call | tf_op jit(solution)/shard_map/pallas_call | solution.py:331
  (1 shorter events, 0.0 us)
